TPU v7x, 32 devices: a whole 2x2x4 slice. The times are simulated.
32 devices in a mesh: grp: 2 (over x), chan: 16 (over z, y, core).
Axes of the slice: x: 2, y: 2, z: 4, core: 2. Of those that a mesh axis runs over, the one named last changes fastest.
Arguments:
- voltages: bfloat16 [8, 16384, 2048], P('grp', 'chan'), parts along dimension 0, may hold values from -6 to 6
- delay_step: int32 [16384], replicated, may hold values from 0 to 1048575
- trials: int32 [256], replicated, may hold values from 0 to 2047
Outputs:
- spectra: float32 [48, 2, 8, 256], P('chan', None, 'grp'), parts along dimension 2
- power: float32 [8, 256], P('grp', 'chan'), parts along dimension 0
There are 2 independent parts, one for each index of `grp`. A program takes and returns all parts, laid end to end along the dimension named above; an argument that names none is the same for every part. Nothing has to cross between parts.
All inputs are finite; a program needn't handle non-finite values.
Results may differ from a plain program's by a relative error of at most 0.0037.
Values may be sent and summed in bfloat16 or wider, within the bound.
A program may use at most 64 MiB of HBM per device.

v0:
```python
import functools
import math

import jax
import jax.numpy as jnp
import numpy as np
from jax import lax
from jax.experimental import pallas as pl
from jax.experimental.pallas import tpu as pltpu
from jax.sharding import PartitionSpec as P

SUBSTEPS = 512
SPIN_DEV = 3
CHUNK = 256
FINE = 64
COARSE = 8
UNROLL = 6
MESH = pl.DeviceIdType.MESH


def padded(count):
    return -(-count // 128) * 128


def build_table(samples, bins):
    index = np.arange(samples)[:, None] * np.arange(bins)[None, :] % samples
    angles = index * (2.0 * math.pi / samples)
    table = np.zeros((samples, padded(2 * bins)), np.float32)
    table[:, :bins] = np.cos(angles)
    table[:, bins : 2 * bins] = -np.sin(angles)
    return jnp.asarray(table.astype(jnp.bfloat16))


def unit_phase(product, shift):
    turns = lax.shift_left(product, jnp.int32(shift)).astype(jnp.float32)
    half = turns * (math.pi * 2.0**-32)
    square = half * half
    sine, cosine = jnp.float32(0), jnp.float32(0)
    for power in (11, 9, 7, 5, 3, 1):
        sine = sine * square + (-1.0) ** (power // 2) / math.factorial(power)
    for power in (12, 10, 8, 6, 4, 2, 0):
        cosine = cosine * square + (-1.0) ** (power // 2) / math.factorial(power)
    sine = sine * half
    return 1.0 - 2.0 * sine * sine, 2.0 * sine * cosine


def kernel(
    n, bins, chan_total, v_ref, table_ref, delay_ref, trials_ref, out_ref, power_ref,
    acc, spec, turn, give, got, mine, bound, came, own, gotp,
    give_send, give_recv, send, recv, power_send, power_recv,
):
    beams, chunk, samples = v_ref.shape
    steps = pl.num_programs(0)
    step = pl.program_id(0)
    shift = 32 - (samples * SUBSTEPS * 2).bit_length() + 1
    delay = delay_ref[...]
    me = lax.axis_index("chan")
    barrier = pltpu.get_barrier_semaphore()

    @pl.when(step == 0)
    def _():
        def greet(hop, carry):
            pl.semaphore_signal(
                barrier, inc=1, device_id={"chan": lax.rem(me + hop, n)}, device_id_type=MESH
            )
            return carry

        lax.fori_loop(1, n, greet, 0)
        acc[...] = jnp.zeros_like(acc)

    bin_delay = lax.broadcasted_iota(jnp.int32, (bins, chunk), 0) * delay
    mid_cos, mid_sin = unit_phase(bin_delay * (samples - 1), shift)
    for jump in range(4):
        jump_cos, jump_sin = unit_phase(bin_delay * (32 * (jump + 1)), shift)
        turn[2 * jump] = jump_cos
        turn[2 * jump + 1] = jump_sin
    for beam in range(beams):
        rows = jnp.dot(v_ref[beam], table_ref[...], preferred_element_type=jnp.float32)
        rows = (rows.T * (1.0 / math.sqrt(samples))).astype(jnp.bfloat16).astype(jnp.float32)
        real, imag = rows[:bins], rows[bins : 2 * bins]
        spec[beam] = real * mid_cos - imag * mid_sin
        spec[beams + beam] = real * mid_sin + imag * mid_cos

    odd = 2 * lax.broadcasted_iota(jnp.int32, (8, chunk), 0) + 1
    fine_rc, fine_rs = unit_phase(odd * delay, shift)
    coarse_rc, coarse_rs = unit_phase(odd * (2 * FINE) * delay, shift)

    def one_bin(spin_bin, carry):
        fc, fs, cc, cs = carry
        cos_rows, sin_rows = [fc], [fs]
        for jump in range(4):
            jc = jnp.broadcast_to(turn[2 * jump, pl.ds(spin_bin, 1), :], (8, chunk))
            js = jnp.broadcast_to(turn[2 * jump + 1, pl.ds(spin_bin, 1), :], (8, chunk))
            a, b, c, d = jc * fc, js * fs, js * fc, jc * fs
            cos_rows.append(a + b)
            sin_rows.append(c - d)
            if jump < 3:
                cos_rows.append(a - b)
                sin_rows.append(c + d)
        fine = jnp.concatenate([x.astype(jnp.bfloat16) for x in _pairs(cos_rows + sin_rows)], 0)
        spectra = [
            jnp.broadcast_to(spec[row, pl.ds(spin_bin, 1), :], (8, chunk))
            for row in range(2 * beams)
        ]
        coarse_rows = [x * cc for x in spectra] + [x * cs for x in spectra]
        coarse = jnp.concatenate([x.astype(jnp.bfloat16) for x in _pairs(coarse_rows)], 0)
        acc[spin_bin] += lax.dot_general(
            coarse, fine, (((1,), (1,)), ((), ())), preferred_element_type=jnp.float32
        )
        return (
            fc * fine_rc - fs * fine_rs,
            fs * fine_rc + fc * fine_rs,
            cc * coarse_rc - cs * coarse_rs,
            cs * coarse_rc + cc * coarse_rs,
        )

    def some_bins(group, carry):
        for offset in range(UNROLL):
            carry = one_bin(group * UNROLL + offset, carry)
        return carry

    one = jnp.ones((8, chunk), jnp.float32)
    zero = jnp.zeros((8, chunk), jnp.float32)
    lax.fori_loop(0, bins // UNROLL, some_bins, (one, zero, one, zero))

    @pl.when(step == steps - 1)
    def _():
        trials = trials_ref[...]
        count = trials.shape[1]
        cell = lax.shift_right_logical(trials, jnp.int32(7))
        fine_odd = 2 * (trials & (2 * FINE - 1)) - (2 * FINE - 1)
        fine_sign = jnp.where(fine_odd > 0, 1.0, -1.0)
        coarse_sign = jnp.where(cell >= COARSE, 1.0, -1.0)
        coarse_index = jnp.where(cell >= COARSE, cell - COARSE, COARSE - 1 - cell)
        row = lax.broadcasted_iota(jnp.int32, (4 * FINE, count), 0) & (2 * FINE - 1)
        block = lax.shift_right_logical(row & (FINE - 1), jnp.int32(3))
        odd_row = 2 * (row & 7) + 1
        jump = lax.shift_right_logical(block + 1, jnp.int32(1)) * 32
        row_odd = jnp.where((block & 1) == 1, jump - odd_row, jump + odd_row)
        hit = row_odd == jnp.abs(fine_odd)
        pick_cos = jnp.where(hit & (row < FINE), 1.0, 0.0)
        pick_sin = jnp.where(hit & (row >= FINE), fine_sign, 0.0)
        pick = jnp.concatenate([pick_cos, pick_sin], 1).astype(jnp.bfloat16)
        scale = 1.0 / math.sqrt(chan_total)
        coarse_hit = lax.broadcasted_iota(jnp.int32, (COARSE, count), 0) == coarse_index
        mask = jnp.where(coarse_hit, scale, 0.0)
        signed = jnp.where(coarse_hit, scale * coarse_sign, 0.0)

        def pick_bin(spin_bin):
            sums = acc[spin_bin]
            high = sums.astype(jnp.bfloat16)
            low = (sums - high.astype(jnp.float32)).astype(jnp.bfloat16)
            picked = jnp.dot(
                jnp.concatenate([high, low], 1), pick, preferred_element_type=jnp.float32
            )
            parts = picked.reshape(2, 2, beams, COARSE, 2 * count)
            cc, cs = parts[0, ..., :count], parts[0, ..., count:]
            sc, ss = parts[1, ..., :count], parts[1, ..., count:]
            even = cc * mask - ss * signed
            odd_part = sc * signed + cs * mask
            real = jnp.sum(even[0] - odd_part[1], axis=1)
            imag = jnp.sum(odd_part[0] + even[1], axis=1)
            return jnp.concatenate([real, imag], 0)

        def pick_owner(owner, target):
            for offset in range(SPIN_DEV):
                target[offset] = pick_bin(owner * SPIN_DEV + offset)

        pairs = n // 2
        sibling = me + 1 - 2 * lax.rem(me, 2)

        def to_sibling(hop):
            return pltpu.make_async_remote_copy(
                src_ref=give.at[hop],
                dst_ref=got.at[hop],
                send_sem=give_send.at[hop],
                recv_sem=give_recv.at[hop],
                device_id={"chan": sibling},
                device_id_type=MESH,
            )

        def to_owner(hop):
            return pltpu.make_async_remote_copy(
                src_ref=bound.at[hop],
                dst_ref=came.at[hop],
                send_sem=send.at[hop],
                recv_sem=recv.at[hop],
                device_id={"chan": lax.rem(me + 2 * hop, n)},
                device_id_type=MESH,
            )

        tile_share = 128 // (count // n)

        def to_power(hop):
            peer = lax.rem(me + hop, n)
            return pltpu.make_async_remote_copy(
                src_ref=own.at[peer // tile_share],
                dst_ref=gotp.at[hop],
                send_sem=power_send.at[hop],
                recv_sem=power_recv.at[hop],
                device_id={"chan": peer},
                device_id_type=MESH,
            )

        pl.semaphore_wait(barrier, n - 1)

        def first(hop, carry):
            slot = lax.rem(hop, pairs)
            pick_owner(lax.rem(sibling + 2 * slot, n), give.at[slot])
            to_sibling(slot).start()
            return carry

        def second(hop, carry):
            pick_owner(lax.rem(me + 2 * hop, n), mine)
            to_sibling(hop).wait_recv()
            whole = mine[...] + got[hop]
            half = jnp.concatenate([whole[..., :128], whole[..., 128:]], 1)
            bound[hop] = half.astype(jnp.bfloat16)
            to_owner(hop).start()
            return carry

        lax.fori_loop(1, pairs + 1, first, 0)
        lax.fori_loop(1, pairs, second, 0)
        pick_owner(me, mine)
        to_sibling(0).wait_recv()
        total = mine[...] + got[0]

        def collect(hop, total):
            to_owner(hop).wait_recv()
            half = came[hop].astype(jnp.float32)
            return total + jnp.concatenate([half[:, : 2 * beams], half[:, 2 * beams :]], 2)

        total = lax.fori_loop(1, pairs, collect, total)
        squares = jnp.sum(total * total, axis=0)
        squares = (squares[:beams] + squares[beams:]) * (1.0 / bins)
        for tile in range(count // 128):
            own[tile] = squares[:, tile * 128 : (tile + 1) * 128]

        def start_power(hop, carry):
            to_power(hop).start()
            return carry

        lax.fori_loop(1, n, start_power, 0)
        out_ref[...] = total

        def collect_power(hop, total):
            to_power(hop).wait_recv()
            return total + gotp[hop]

        power_ref[...] = lax.fori_loop(1, n, collect_power, own[me // tile_share])

        def finish_power(hop, carry):
            to_power(hop).wait_send()
            return carry

        def finish(hop, carry):
            to_owner(hop).wait_send()
            to_sibling(hop).wait_send()
            return carry

        lax.fori_loop(1, n, finish_power, 0)
        lax.fori_loop(1, pairs, finish, 0)
        to_sibling(0).wait_send()


def finish_kernel(n, spectra_ref, power_ref, out_ref, own_ref):
    beams, lanes = own_ref.shape
    out_ref[...] = spectra_ref[...].reshape(out_ref.shape)
    place = lax.rem(lax.axis_index("chan"), 128 // lanes)
    power = power_ref[...]
    total = jnp.zeros((beams, lanes), jnp.float32)
    for index in range(128 // lanes):
        total = jnp.where(place == index, power[:, index * lanes : (index + 1) * lanes], total)
    own_ref[...] = total


def _pairs(rows):
    return [jnp.concatenate(rows[i : i + 2], 0) for i in range(0, len(rows), 2)]


def per_device(voltages, delay_step, trials):
    beams, local_chan, samples = voltages.shape
    n = lax.axis_size("chan")
    bins = SPIN_DEV * n
    chan_total = delay_step.shape[0]
    count = trials.shape[0]
    table = build_table(samples, bins)
    chunk = min(CHUNK, local_chan)
    steps = local_chan // chunk
    rows = 2 * beams
    vmem = pltpu.VMEM
    spectra, power = pl.pallas_call(
        functools.partial(kernel, n, bins, chan_total),
        out_shape=(
            jax.ShapeDtypeStruct((SPIN_DEV, rows, count), jnp.float32),
            jax.ShapeDtypeStruct((beams, 128), jnp.float32),
        ),
        grid=(steps,),
        in_specs=[
            pl.BlockSpec((beams, chunk, samples), lambda i: (0, i, 0)),
            pl.BlockSpec(table.shape, lambda i: (0, 0)),
            pl.BlockSpec((1, chunk), lambda i: (0, lax.axis_index("chan") * steps + i)),
            pl.BlockSpec((1, count), lambda i: (0, 0)),
        ],
        out_specs=(
            pl.BlockSpec((SPIN_DEV, rows, count), lambda i: (0, 0, 0)),
            pl.BlockSpec((beams, 128), lambda i: (0, 0)),
        ),
        scratch_shapes=[
            vmem((bins, 2 * rows * COARSE, 2 * FINE), jnp.float32),
            vmem((rows, bins, chunk), jnp.float32),
            vmem((8, bins, chunk), jnp.float32),
            vmem((n // 2, SPIN_DEV, rows, count), jnp.float32),
            vmem((n // 2, SPIN_DEV, rows, count), jnp.float32),
            vmem((SPIN_DEV, rows, count), jnp.float32),
            vmem((n // 2, SPIN_DEV, 2 * rows, count // 2), jnp.bfloat16),
            vmem((n // 2, SPIN_DEV, 2 * rows, count // 2), jnp.bfloat16),
            vmem((count // 128, beams, 128), jnp.float32),
            vmem((n, beams, 128), jnp.float32),
            pltpu.SemaphoreType.DMA((n // 2,)),
            pltpu.SemaphoreType.DMA((n // 2,)),
            pltpu.SemaphoreType.DMA((n // 2,)),
            pltpu.SemaphoreType.DMA((n // 2,)),
            pltpu.SemaphoreType.DMA((n,)),
            pltpu.SemaphoreType.DMA((n,)),
        ],
        compiler_params=pltpu.CompilerParams(
            dimension_semantics=("arbitrary",),
            vmem_limit_bytes=56 * 1024 * 1024,
            collective_id=0,
            has_side_effects=True,
        ),
    )(voltages, table, delay_step.reshape(1, chan_total), trials.reshape(1, count))
    return pl.pallas_call(
        functools.partial(finish_kernel, n),
        out_shape=(
            jax.ShapeDtypeStruct((SPIN_DEV, 2, beams, count), jnp.float32),
            jax.ShapeDtypeStruct((beams, count // n), jnp.float32),
        ),
    )(spectra, power)


def solution(mesh):
    return jax.shard_map(
        per_device,
        mesh=mesh,
        in_specs=(P("grp", "chan", None), P(), P()),
        out_specs=(P("chan", None, "grp", None), P("grp", "chan")),
        check_vma=False,
    )
```

profile of v0, /device:TPU:0, one launch (start us, length us, event | category | flops | bytes accessed | tf_op | source)
XLA Modules:
  0.0 36.3 jit_solution(10862219095469014754)
XLA Ops:
  0.6 33.8 %shard_map.59 = (f32[3,8,256]{2,1,0:T(8,128)}, f32[4,128]{1,0:T(4,128)}) custom-call(bf16[4,1024,2048]{2,1,0:T(8,128)(2,1)} %v_ref.1, bf16[2048,128]{1,0:T(8,128)(2,1)} %constant.2.clone.table_ref, s32[1,16384]{1,0:T(1,128)} %bitcast.2, s32[1,256]{1,0:T(1,128)} %bitcast.3), custom_call_target="tpu_custom_call" | custom-call | tf_op jit(solution)/shard_map/pallas_call | solution.py:292
  34.4 1.9 %shard_map.60 = (f32[3,2,4,256]{3,2,1,0:T(4,128)}, f32[4,16]{1,0:T(4,128)}) custom-call(f32[3,8,256]{2,1,0:T(8,128)} %get-tuple-element.4.spectra_ref, f32[4,128]{1,0:T(4,128)} %get-tuple-element.5.power_ref), custom_call_target="tpu_custom_call" | custom-call | tf_op jit(solution)/shard_map/pallas_call | solution.py:334
where the time goes:
time: 36.4 us; the launch traced here: 36.3 us
  Pallas kernels  35.6 us (98%)
  between operations  0.64 us (2%)
    pallas_call x1, Pallas kernels, per_device(): pl.pallas_call(functools.partial(kernel, n, bins, chan_total), out_shape=...  33.8 us
    pallas_call x1, Pallas kernels, per_device(): pl.pallas_call(functools.partial(finish_kernel, n), out_shape=(jax.ShapeD...  1.87 us

commit v1 on v0

--- a/solution.py
+++ b/solution.py
@@ -14,7 +14,6 @@
 CHUNK = 256
 FINE = 64
 COARSE = 8
-UNROLL = 6
 MESH = pl.DeviceIdType.MESH
 
 
@@ -45,15 +44,14 @@
 
 
 def kernel(
-    n, bins, chan_total, v_ref, table_ref, delay_ref, trials_ref, out_ref, power_ref,
-    acc, spec, turn, give, got, mine, bound, came, own, gotp,
+    n, bins, chan_total, v_ref, table_ref, delay_ref, full_ref, trials_ref, out_ref, power_ref,
+    spec, turn, give, got, mine, bound, came, own, gotp,
     give_send, give_recv, send, recv, power_send, power_recv,
 ):
     beams, chunk, samples = v_ref.shape
     steps = pl.num_programs(0)
     step = pl.program_id(0)
     shift = 32 - (samples * SUBSTEPS * 2).bit_length() + 1
-    delay = delay_ref[...]
     me = lax.axis_index("chan")
     barrier = pltpu.get_barrier_semaphore()
 
@@ -66,31 +64,28 @@
             return carry
 
         lax.fori_loop(1, n, greet, 0)
-        acc[...] = jnp.zeros_like(acc)
-
-    bin_delay = lax.broadcasted_iota(jnp.int32, (bins, chunk), 0) * delay
+
+    here = pl.ds(pl.multiple_of(step * chunk, chunk), chunk)
+    bin_delay = lax.broadcasted_iota(jnp.int32, (bins, chunk), 0) * delay_ref[...]
     mid_cos, mid_sin = unit_phase(bin_delay * (samples - 1), shift)
     for jump in range(4):
         jump_cos, jump_sin = unit_phase(bin_delay * (32 * (jump + 1)), shift)
-        turn[2 * jump] = jump_cos
-        turn[2 * jump + 1] = jump_sin
+        turn[2 * jump, :, here] = jump_cos
+        turn[2 * jump + 1, :, here] = jump_sin
     for beam in range(beams):
         rows = jnp.dot(v_ref[beam], table_ref[...], preferred_element_type=jnp.float32)
         rows = (rows.T * (1.0 / math.sqrt(samples))).astype(jnp.bfloat16).astype(jnp.float32)
         real, imag = rows[:bins], rows[bins : 2 * bins]
-        spec[beam] = real * mid_cos - imag * mid_sin
-        spec[beams + beam] = real * mid_sin + imag * mid_cos
-
-    odd = 2 * lax.broadcasted_iota(jnp.int32, (8, chunk), 0) + 1
-    fine_rc, fine_rs = unit_phase(odd * delay, shift)
-    coarse_rc, coarse_rs = unit_phase(odd * (2 * FINE) * delay, shift)
-
-    def one_bin(spin_bin, carry):
-        fc, fs, cc, cs = carry
+        spec[beam, :, here] = real * mid_cos - imag * mid_sin
+        spec[beams + beam, :, here] = real * mid_sin + imag * mid_cos
+
+    def bin_sums(spin_bin, lanes, fc, fs, cc, cs):
+        def spread(ref, row):
+            return jnp.broadcast_to(ref[row, pl.ds(spin_bin, 1), lanes], (8, chunk))
+
         cos_rows, sin_rows = [fc], [fs]
         for jump in range(4):
-            jc = jnp.broadcast_to(turn[2 * jump, pl.ds(spin_bin, 1), :], (8, chunk))
-            js = jnp.broadcast_to(turn[2 * jump + 1, pl.ds(spin_bin, 1), :], (8, chunk))
+            jc, js = spread(turn, 2 * jump), spread(turn, 2 * jump + 1)
             a, b, c, d = jc * fc, js * fs, js * fc, jc * fs
             cos_rows.append(a + b)
             sin_rows.append(c - d)
@@ -98,30 +93,31 @@
                 cos_rows.append(a - b)
                 sin_rows.append(c + d)
         fine = jnp.concatenate([x.astype(jnp.bfloat16) for x in _pairs(cos_rows + sin_rows)], 0)
-        spectra = [
-            jnp.broadcast_to(spec[row, pl.ds(spin_bin, 1), :], (8, chunk))
-            for row in range(2 * beams)
-        ]
+        spectra = [spread(spec, row) for row in range(2 * beams)]
         coarse_rows = [x * cc for x in spectra] + [x * cs for x in spectra]
         coarse = jnp.concatenate([x.astype(jnp.bfloat16) for x in _pairs(coarse_rows)], 0)
-        acc[spin_bin] += lax.dot_general(
+        return lax.dot_general(
             coarse, fine, (((1,), (1,)), ((), ())), preferred_element_type=jnp.float32
         )
-        return (
-            fc * fine_rc - fs * fine_rs,
-            fs * fine_rc + fc * fine_rs,
-            cc * coarse_rc - cs * coarse_rs,
-            cs * coarse_rc + cc * coarse_rs,
-        )
-
-    def some_bins(group, carry):
-        for offset in range(UNROLL):
-            carry = one_bin(group * UNROLL + offset, carry)
-        return carry
-
-    one = jnp.ones((8, chunk), jnp.float32)
-    zero = jnp.zeros((8, chunk), jnp.float32)
-    lax.fori_loop(0, bins // UNROLL, some_bins, (one, zero, one, zero))
+
+    def owner_sums(owner):
+        odd = 2 * lax.broadcasted_iota(jnp.int32, (8, chunk), 0) + 1
+        sums = [0.0] * SPIN_DEV
+        for block in range(spec.shape[2] // chunk):
+            lanes = slice(block * chunk, (block + 1) * chunk)
+            fine_step = odd * full_ref[:, lanes]
+            coarse_step = fine_step * (2 * FINE)
+            fine_rc, fine_rs = unit_phase(fine_step, shift)
+            coarse_rc, coarse_rs = unit_phase(coarse_step, shift)
+            fc, fs = unit_phase(fine_step * (owner * SPIN_DEV), shift)
+            cc, cs = unit_phase(coarse_step * (owner * SPIN_DEV), shift)
+            for offset in range(SPIN_DEV):
+                spin_bin = owner * SPIN_DEV + offset
+                sums[offset] += bin_sums(spin_bin, lanes, fc, fs, cc, cs)
+                if offset < SPIN_DEV - 1:
+                    fc, fs = fc * fine_rc - fs * fine_rs, fs * fine_rc + fc * fine_rs
+                    cc, cs = cc * coarse_rc - cs * coarse_rs, cs * coarse_rc + cc * coarse_rs
+        return sums
 
     @pl.when(step == steps - 1)
     def _():
@@ -146,8 +142,7 @@
         mask = jnp.where(coarse_hit, scale, 0.0)
         signed = jnp.where(coarse_hit, scale * coarse_sign, 0.0)
 
-        def pick_bin(spin_bin):
-            sums = acc[spin_bin]
+        def pick_bin(sums):
             high = sums.astype(jnp.bfloat16)
             low = (sums - high.astype(jnp.float32)).astype(jnp.bfloat16)
             picked = jnp.dot(
@@ -156,15 +151,14 @@
             parts = picked.reshape(2, 2, beams, COARSE, 2 * count)
             cc, cs = parts[0, ..., :count], parts[0, ..., count:]
             sc, ss = parts[1, ..., :count], parts[1, ..., count:]
-            even = cc * mask - ss * signed
-            odd_part = sc * signed + cs * mask
-            real = jnp.sum(even[0] - odd_part[1], axis=1)
-            imag = jnp.sum(odd_part[0] + even[1], axis=1)
+            real = (cc[0] - cs[1]) * mask - (ss[0] + sc[1]) * signed
+            imag = (cs[0] + cc[1]) * mask + (sc[0] - ss[1]) * signed
+            real, imag = jnp.sum(real, axis=1), jnp.sum(imag, axis=1)
             return jnp.concatenate([real, imag], 0)
 
         def pick_owner(owner, target):
-            for offset in range(SPIN_DEV):
-                target[offset] = pick_bin(owner * SPIN_DEV + offset)
+            for offset, sums in enumerate(owner_sums(owner)):
+                target[offset] = pick_bin(sums)
 
         pairs = n // 2
         sibling = me + 1 - 2 * lax.rem(me, 2)
@@ -211,18 +205,21 @@
             return carry
 
         def second(hop, carry):
-            pick_owner(lax.rem(me + 2 * hop, n), mine)
-            to_sibling(hop).wait_recv()
-            whole = mine[...] + got[hop]
-            half = jnp.concatenate([whole[..., :128], whole[..., 128:]], 1)
-            bound[hop] = half.astype(jnp.bfloat16)
-            to_owner(hop).start()
+            slot = lax.rem(hop, pairs)
+            pick_owner(lax.rem(me + 2 * slot, n), mine)
+            to_sibling(slot).wait_recv()
+
+            @pl.when(hop < pairs)
+            def _():
+                whole = mine[...] + got[hop]
+                half = jnp.concatenate([whole[..., :128], whole[..., 128:]], 1)
+                bound[hop] = half.astype(jnp.bfloat16)
+                to_owner(hop).start()
+
             return carry
 
         lax.fori_loop(1, pairs + 1, first, 0)
-        lax.fori_loop(1, pairs, second, 0)
-        pick_owner(me, mine)
-        to_sibling(0).wait_recv()
+        lax.fori_loop(1, pairs + 1, second, 0)
         total = mine[...] + got[0]
 
         def collect(hop, total):
@@ -288,6 +285,7 @@
     chunk = min(CHUNK, local_chan)
     steps = local_chan // chunk
     rows = 2 * beams
+    delay = delay_step.reshape(1, chan_total)
     vmem = pltpu.VMEM
     spectra, power = pl.pallas_call(
         functools.partial(kernel, n, bins, chan_total),
@@ -300,6 +298,7 @@
             pl.BlockSpec((beams, chunk, samples), lambda i: (0, i, 0)),
             pl.BlockSpec(table.shape, lambda i: (0, 0)),
             pl.BlockSpec((1, chunk), lambda i: (0, lax.axis_index("chan") * steps + i)),
+            pl.BlockSpec((1, local_chan), lambda i: (0, lax.axis_index("chan"))),
             pl.BlockSpec((1, count), lambda i: (0, 0)),
         ],
         out_specs=(
@@ -307,9 +306,8 @@
             pl.BlockSpec((beams, 128), lambda i: (0, 0)),
         ),
         scratch_shapes=[
-            vmem((bins, 2 * rows * COARSE, 2 * FINE), jnp.float32),
-            vmem((rows, bins, chunk), jnp.float32),
-            vmem((8, bins, chunk), jnp.float32),
+            vmem((rows, bins, local_chan), jnp.float32),
+            vmem((8, bins, local_chan), jnp.float32),
             vmem((n // 2, SPIN_DEV, rows, count), jnp.float32),
             vmem((n // 2, SPIN_DEV, rows, count), jnp.float32),
             vmem((SPIN_DEV, rows, count), jnp.float32),
@@ -330,7 +328,7 @@
             collective_id=0,
             has_side_effects=True,
         ),
-    )(voltages, table, delay_step.reshape(1, chan_total), trials.reshape(1, count))
+    )(voltages, table, delay, delay, trials.reshape(1, count))
     return pl.pallas_call(
         functools.partial(finish_kernel, n),
         out_shape=(

time: 36.4 us -> 36.7 us (level)
  no operation moved by 1% of the time
where the time goes in v1:
time: 36.7 us; the launch traced here: 36.5 us
  Pallas kernels  35.9 us (98%)
  between operations  0.64 us (2%)
    pallas_call x1, Pallas kernels, per_device(): pl.pallas_call(functools.partial(kernel, n, bins, chan_total), out_shape=...  34 us
    pallas_call x1, Pallas kernels, per_device(): pl.pallas_call(functools.partial(finish_kernel, n), out_shape=(jax.ShapeD...  1.87 us

profile of v1, /device:TPU:0, one launch (start us, length us, event | category | flops | bytes accessed | tf_op | source)
XLA Modules:
  0.0 36.5 jit_solution(990790629745279561)
XLA Ops:
  0.6 34.0 %shard_map.59 = (f32[3,8,256]{2,1,0:T(8,128)}, f32[4,128]{1,0:T(4,128)}) custom-call(bf16[4,1024,2048]{2,1,0:T(8,128)(2,1)} %v_ref.1, bf16[2048,128]{1,0:T(8,128)(2,1)} %constant.2.clone.table_ref, s32[1,16384]{1,0:T(1,128)} %bitcast.2, s32[1,16384]{1,0:T(1,128)} %bitcast.3, s32[1,256]{1,0:T(1,128)} %bitcast.4), custom_call_target="tpu_custom_call" | custom-call | tf_op jit(solution)/shard_map/pallas_call | solution.py:290
  34.7 1.9 %shard_map.60 = (f32[3,2,4,256]{3,2,1,0:T(4,128)}, f32[4,16]{1,0:T(4,128)}) custom-call(f32[3,8,256]{2,1,0:T(8,128)} %get-tuple-element.4.spectra_ref, f32[4,128]{1,0:T(4,128)} %get-tuple-element.5.power_ref), custom_call_target="tpu_custom_call" | custom-call | tf_op jit(solution)/shard_map/pallas_call | solution.py:332

commit v2 on v1

--- a/solution.py
+++ b/solution.py
@@ -44,8 +44,8 @@
 
 
 def kernel(
-    n, bins, chan_total, v_ref, table_ref, delay_ref, full_ref, trials_ref, out_ref, power_ref,
-    spec, turn, give, got, mine, bound, came, own, gotp,
+    n, bins, chan_total, v_ref, table_ref, delay_ref, trials_ref, out_ref, power_ref,
+    spec, fine, coarse, give, got, mine, bound, came, own, gotp,
     give_send, give_recv, send, recv, power_send, power_recv,
 ):
     beams, chunk, samples = v_ref.shape
@@ -68,10 +68,6 @@
     here = pl.ds(pl.multiple_of(step * chunk, chunk), chunk)
     bin_delay = lax.broadcasted_iota(jnp.int32, (bins, chunk), 0) * delay_ref[...]
     mid_cos, mid_sin = unit_phase(bin_delay * (samples - 1), shift)
-    for jump in range(4):
-        jump_cos, jump_sin = unit_phase(bin_delay * (32 * (jump + 1)), shift)
-        turn[2 * jump, :, here] = jump_cos
-        turn[2 * jump + 1, :, here] = jump_sin
     for beam in range(beams):
         rows = jnp.dot(v_ref[beam], table_ref[...], preferred_element_type=jnp.float32)
         rows = (rows.T * (1.0 / math.sqrt(samples))).astype(jnp.bfloat16).astype(jnp.float32)
@@ -79,44 +75,41 @@
         spec[beam, :, here] = real * mid_cos - imag * mid_sin
         spec[beams + beam, :, here] = real * mid_sin + imag * mid_cos
 
-    def bin_sums(spin_bin, lanes, fc, fs, cc, cs):
-        def spread(ref, row):
-            return jnp.broadcast_to(ref[row, pl.ds(spin_bin, 1), lanes], (8, chunk))
-
-        cos_rows, sin_rows = [fc], [fs]
-        for jump in range(4):
-            jc, js = spread(turn, 2 * jump), spread(turn, 2 * jump + 1)
-            a, b, c, d = jc * fc, js * fs, js * fc, jc * fs
-            cos_rows.append(a + b)
-            sin_rows.append(c - d)
-            if jump < 3:
-                cos_rows.append(a - b)
-                sin_rows.append(c + d)
-        fine = jnp.concatenate([x.astype(jnp.bfloat16) for x in _pairs(cos_rows + sin_rows)], 0)
-        spectra = [spread(spec, row) for row in range(2 * beams)]
-        coarse_rows = [x * cc for x in spectra] + [x * cs for x in spectra]
-        coarse = jnp.concatenate([x.astype(jnp.bfloat16) for x in _pairs(coarse_rows)], 0)
-        return lax.dot_general(
-            coarse, fine, (((1,), (1,)), ((), ())), preferred_element_type=jnp.float32
-        )
+    column = jnp.broadcast_to(delay_ref[...].astype(jnp.float32), (2 * FINE, chunk)).T
+    lane = lax.broadcasted_iota(jnp.int32, (chunk, 2 * FINE), 1)
+    odd_lane = 2 * (lane & (FINE - 1)) + 1
+    fine_cos, fine_sin = unit_phase(odd_lane * column.astype(jnp.int32), shift)
+    fine[0, here] = jnp.where(lane < FINE, fine_cos, -fine_sin)
+    fine[1, here] = jnp.where(lane < FINE, 1.0, 0.0)
+    fine[2, here] = 2.0 * fine_cos
+    odd_row = 2 * lax.broadcasted_iota(jnp.int32, (COARSE, chunk), 0) + 1
+    coarse_cos, coarse_sin = unit_phase(odd_row * (2 * FINE) * delay_ref[...], shift)
+    coarse[0, :, here] = jnp.ones_like(coarse_cos)
+    coarse[1, :, here] = jnp.zeros_like(coarse_cos)
+    coarse[2, :, here] = coarse_cos
+    coarse[3, :, here] = coarse_sin
 
     def owner_sums(owner):
-        odd = 2 * lax.broadcasted_iota(jnp.int32, (8, chunk), 0) + 1
         sums = [0.0] * SPIN_DEV
         for block in range(spec.shape[2] // chunk):
             lanes = slice(block * chunk, (block + 1) * chunk)
-            fine_step = odd * full_ref[:, lanes]
-            coarse_step = fine_step * (2 * FINE)
-            fine_rc, fine_rs = unit_phase(fine_step, shift)
-            coarse_rc, coarse_rs = unit_phase(coarse_step, shift)
-            fc, fs = unit_phase(fine_step * (owner * SPIN_DEV), shift)
-            cc, cs = unit_phase(coarse_step * (owner * SPIN_DEV), shift)
+            before, now, twice = fine[0, lanes], fine[1, lanes], fine[2, lanes]
+            cc, cs, turn_c, turn_s = (coarse[index, :, lanes] for index in range(4))
             for offset in range(SPIN_DEV):
                 spin_bin = owner * SPIN_DEV + offset
-                sums[offset] += bin_sums(spin_bin, lanes, fc, fs, cc, cs)
-                if offset < SPIN_DEV - 1:
-                    fc, fs = fc * fine_rc - fs * fine_rs, fs * fine_rc + fc * fine_rs
-                    cc, cs = cc * coarse_rc - cs * coarse_rs, cs * coarse_rc + cc * coarse_rs
+                spectra = [
+                    jnp.broadcast_to(spec[row, pl.ds(spin_bin, 1), lanes], (8, chunk))
+                    for row in range(2 * beams)
+                ]
+                rows = [x * cc for x in spectra] + [x * cs for x in spectra]
+                rows = jnp.concatenate([x.astype(jnp.bfloat16) for x in _pairs(rows)], 0)
+                sums[offset] += jnp.dot(
+                    rows, now.astype(jnp.bfloat16), preferred_element_type=jnp.float32
+                )
+                before, now = now, twice * now - before
+                cc, cs = cc * turn_c - cs * turn_s, cs * turn_c + cc * turn_s
+            fine[0, lanes], fine[1, lanes] = before, now
+            coarse[0, :, lanes], coarse[1, :, lanes] = cc, cs
         return sums
 
     @pl.when(step == steps - 1)
@@ -129,10 +122,7 @@
         coarse_sign = jnp.where(cell >= COARSE, 1.0, -1.0)
         coarse_index = jnp.where(cell >= COARSE, cell - COARSE, COARSE - 1 - cell)
         row = lax.broadcasted_iota(jnp.int32, (4 * FINE, count), 0) & (2 * FINE - 1)
-        block = lax.shift_right_logical(row & (FINE - 1), jnp.int32(3))
-        odd_row = 2 * (row & 7) + 1
-        jump = lax.shift_right_logical(block + 1, jnp.int32(1)) * 32
-        row_odd = jnp.where((block & 1) == 1, jump - odd_row, jump + odd_row)
+        row_odd = 2 * (row & (FINE - 1)) + 1
         hit = row_odd == jnp.abs(fine_odd)
         pick_cos = jnp.where(hit & (row < FINE), 1.0, 0.0)
         pick_sin = jnp.where(hit & (row >= FINE), fine_sign, 0.0)
@@ -156,12 +146,10 @@
             real, imag = jnp.sum(real, axis=1), jnp.sum(imag, axis=1)
             return jnp.concatenate([real, imag], 0)
 
-        def pick_owner(owner, target):
-            for offset, sums in enumerate(owner_sums(owner)):
-                target[offset] = pick_bin(sums)
-
         pairs = n // 2
-        sibling = me + 1 - 2 * lax.rem(me, 2)
+        side = lax.rem(me, 2)
+        sibling = me + 1 - 2 * side
+        my_pair = me // 2
 
         def to_sibling(hop):
             return pltpu.make_async_remote_copy(
@@ -173,13 +161,13 @@
                 device_id_type=MESH,
             )
 
-        def to_owner(hop):
+        def to_owner(pair, slot):
             return pltpu.make_async_remote_copy(
-                src_ref=bound.at[hop],
-                dst_ref=came.at[hop],
-                send_sem=send.at[hop],
-                recv_sem=recv.at[hop],
-                device_id={"chan": lax.rem(me + 2 * hop, n)},
+                src_ref=bound.at[pair],
+                dst_ref=came.at[slot],
+                send_sem=send.at[pair],
+                recv_sem=recv.at[slot],
+                device_id={"chan": 2 * pair + side},
                 device_id_type=MESH,
             )
 
@@ -198,36 +186,41 @@
 
         pl.semaphore_wait(barrier, n - 1)
 
-        def first(hop, carry):
-            slot = lax.rem(hop, pairs)
-            pick_owner(lax.rem(sibling + 2 * slot, n), give.at[slot])
-            to_sibling(slot).start()
-            return carry
-
-        def second(hop, carry):
-            slot = lax.rem(hop, pairs)
-            pick_owner(lax.rem(me + 2 * slot, n), mine)
-            to_sibling(slot).wait_recv()
-
-            @pl.when(hop < pairs)
+        def pass_on(pair):
+            to_sibling(pair).wait_recv()
+            whole = mine[pair] + got[pair]
+            mine[pair] = whole
+
+            @pl.when(pair != my_pair)
             def _():
-                whole = mine[...] + got[hop]
                 half = jnp.concatenate([whole[..., :128], whole[..., 128:]], 1)
-                bound[hop] = half.astype(jnp.bfloat16)
-                to_owner(hop).start()
-
-            return carry
-
-        lax.fori_loop(1, pairs + 1, first, 0)
-        lax.fori_loop(1, pairs + 1, second, 0)
-        total = mine[...] + got[0]
+                bound[pair] = half.astype(jnp.bfloat16)
+                to_owner(pair, my_pair).start()
+
+        def one_pair(pair, carry):
+            even = [pick_bin(sums) for sums in owner_sums(2 * pair)]
+            odd = [pick_bin(sums) for sums in owner_sums(2 * pair + 1)]
+            for offset in range(SPIN_DEV):
+                give[pair, offset] = jnp.where(side == 0, odd[offset], even[offset])
+                mine[pair, offset] = jnp.where(side == 0, even[offset], odd[offset])
+            to_sibling(pair).start()
+
+            @pl.when(pair > 0)
+            def _():
+                pass_on(pair - 1)
+
+            return carry
+
+        lax.fori_loop(0, pairs, one_pair, 0)
+        pass_on(pairs - 1)
 
         def collect(hop, total):
-            to_owner(hop).wait_recv()
-            half = came[hop].astype(jnp.float32)
+            slot = lax.rem(my_pair + hop, pairs)
+            to_owner(slot, slot).wait_recv()
+            half = came[slot].astype(jnp.float32)
             return total + jnp.concatenate([half[:, : 2 * beams], half[:, 2 * beams :]], 2)
 
-        total = lax.fori_loop(1, pairs, collect, total)
+        total = lax.fori_loop(1, pairs, collect, mine[my_pair])
         squares = jnp.sum(total * total, axis=0)
         squares = (squares[:beams] + squares[beams:]) * (1.0 / bins)
         for tile in range(count // 128):
@@ -251,13 +244,14 @@
             return carry
 
         def finish(hop, carry):
-            to_owner(hop).wait_send()
-            to_sibling(hop).wait_send()
+            pair = lax.rem(my_pair + hop, pairs)
+            to_owner(pair, my_pair).wait_send()
+            to_sibling(pair).wait_send()
             return carry
 
         lax.fori_loop(1, n, finish_power, 0)
         lax.fori_loop(1, pairs, finish, 0)
-        to_sibling(0).wait_send()
+        to_sibling(my_pair).wait_send()
 
 
 def finish_kernel(n, spectra_ref, power_ref, out_ref, own_ref):
@@ -298,7 +292,6 @@
             pl.BlockSpec((beams, chunk, samples), lambda i: (0, i, 0)),
             pl.BlockSpec(table.shape, lambda i: (0, 0)),
             pl.BlockSpec((1, chunk), lambda i: (0, lax.axis_index("chan") * steps + i)),
-            pl.BlockSpec((1, local_chan), lambda i: (0, lax.axis_index("chan"))),
             pl.BlockSpec((1, count), lambda i: (0, 0)),
         ],
         out_specs=(
@@ -307,10 +300,11 @@
         ),
         scratch_shapes=[
             vmem((rows, bins, local_chan), jnp.float32),
-            vmem((8, bins, local_chan), jnp.float32),
+            vmem((3, local_chan, 2 * FINE), jnp.float32),
+            vmem((4, COARSE, local_chan), jnp.float32),
             vmem((n // 2, SPIN_DEV, rows, count), jnp.float32),
             vmem((n // 2, SPIN_DEV, rows, count), jnp.float32),
-            vmem((SPIN_DEV, rows, count), jnp.float32),
+            vmem((n // 2, SPIN_DEV, rows, count), jnp.float32),
             vmem((n // 2, SPIN_DEV, 2 * rows, count // 2), jnp.bfloat16),
             vmem((n // 2, SPIN_DEV, 2 * rows, count // 2), jnp.bfloat16),
             vmem((count // 128, beams, 128), jnp.float32),
@@ -328,7 +322,7 @@
             collective_id=0,
             has_side_effects=True,
         ),
-    )(voltages, table, delay, delay, trials.reshape(1, count))
+    )(voltages, table, delay, trials.reshape(1, count))
     return pl.pallas_call(
         functools.partial(finish_kernel, n),
         out_shape=(

time: 36.7 us -> 34.1 us (0.929)
  Pallas kernels: 35.9 us -> 33.3 us
    pallas_call x1, Pallas kernels: 34 us -> 31.4 us  [per_device(): pl.pallas_call(functools.partial(kernel, n, bins, chan_total), out_shape=...]
where the time goes in v2:
time: 34.1 us; the launch traced here: 33.9 us
  Pallas kernels  33.3 us (98%)
  between operations  0.64 us (2%)
    pallas_call x1, Pallas kernels, per_device(): pl.pallas_call(functools.partial(kernel, n, bins, chan_total), out_shape=...  31.4 us
    pallas_call x1, Pallas kernels, per_device(): pl.pallas_call(functools.partial(finish_kernel, n), out_shape=(jax.ShapeD...  1.87 us

profile of v2, /device:TPU:0, one launch (start us, length us, event | category | flops | bytes accessed | tf_op | source)
XLA Modules:
  0.0 33.9 jit_solution(15115189279395866040)
XLA Ops:
  0.6 31.4 %shard_map.59 = (f32[3,8,256]{2,1,0:T(8,128)}, f32[4,128]{1,0:T(4,128)}) custom-call(bf16[4,1024,2048]{2,1,0:T(8,128)(2,1)} %v_ref.1, bf16[2048,128]{1,0:T(8,128)(2,1)} %constant.2.clone.table_ref, s32[1,16384]{1,0:T(1,128)} %bitcast.2, s32[1,256]{1,0:T(1,128)} %bitcast.3), custom_call_target="tpu_custom_call" | custom-call | tf_op jit(solution)/shard_map/pallas_call | solution.py:284
  32.1 1.9 %shard_map.60 = (f32[3,2,4,256]{3,2,1,0:T(4,128)}, f32[4,16]{1,0:T(4,128)}) custom-call(f32[3,8,256]{2,1,0:T(8,128)} %get-tuple-element.4.spectra_ref, f32[4,128]{1,0:T(4,128)} %get-tuple-element.5.power_ref), custom_call_target="tpu_custom_call" | custom-call | tf_op jit(solution)/shard_map/pallas_call | solution.py:326

commit v3 on v2

--- a/solution.py
+++ b/solution.py
@@ -45,7 +45,7 @@
 
 def kernel(
     n, bins, chan_total, v_ref, table_ref, delay_ref, trials_ref, out_ref, power_ref,
-    spec, fine, coarse, give, got, mine, bound, came, own, gotp,
+    spec, fine, coarse, left_a, right_a, left_b, right_b, give, got, mine, bound, came, own, gotp,
     give_send, give_recv, send, recv, power_send, power_recv,
 ):
     beams, chunk, samples = v_ref.shape
@@ -68,12 +68,17 @@
     here = pl.ds(pl.multiple_of(step * chunk, chunk), chunk)
     bin_delay = lax.broadcasted_iota(jnp.int32, (bins, chunk), 0) * delay_ref[...]
     mid_cos, mid_sin = unit_phase(bin_delay * (samples - 1), shift)
+    every = v_ref[...].reshape(beams * chunk, samples)
+    every = jnp.dot(every, table_ref[...], preferred_element_type=jnp.float32)
     for beam in range(beams):
-        rows = jnp.dot(v_ref[beam], table_ref[...], preferred_element_type=jnp.float32)
-        rows = (rows.T * (1.0 / math.sqrt(samples))).astype(jnp.bfloat16).astype(jnp.float32)
+        rows = every[beam * chunk : (beam + 1) * chunk].T
+        rows = (rows * (1.0 / math.sqrt(samples))).astype(jnp.bfloat16).astype(jnp.float32)
         real, imag = rows[:bins], rows[bins : 2 * bins]
-        spec[beam, :, here] = real * mid_cos - imag * mid_sin
-        spec[beams + beam, :, here] = real * mid_sin + imag * mid_cos
+        turned = real * mid_cos - imag * mid_sin, real * mid_sin + imag * mid_cos
+        for kind, values in enumerate(turned):
+            place = pl.ds(kind * beams + beam, bins, stride=2 * beams)
+            for tile in range(chunk // 128):
+                spec[step * (chunk // 128) + tile, place, :] = values[:, tile * 128 : tile * 128 + 128]
 
     column = jnp.broadcast_to(delay_ref[...].astype(jnp.float32), (2 * FINE, chunk)).T
     lane = lax.broadcasted_iota(jnp.int32, (chunk, 2 * FINE), 1)
@@ -89,28 +94,39 @@
     coarse[2, :, here] = coarse_cos
     coarse[3, :, here] = coarse_sin
 
-    def owner_sums(owner):
-        sums = [0.0] * SPIN_DEV
-        for block in range(spec.shape[2] // chunk):
-            lanes = slice(block * chunk, (block + 1) * chunk)
-            before, now, twice = fine[0, lanes], fine[1, lanes], fine[2, lanes]
+    def build(owner, left, right):
+        for tile in range(spec.shape[0]):
+            start = tile * 128
+            lanes = slice(start, start + 128)
             cc, cs, turn_c, turn_s = (coarse[index, :, lanes] for index in range(4))
             for offset in range(SPIN_DEV):
-                spin_bin = owner * SPIN_DEV + offset
-                spectra = [
-                    jnp.broadcast_to(spec[row, pl.ds(spin_bin, 1), lanes], (8, chunk))
-                    for row in range(2 * beams)
-                ]
-                rows = [x * cc for x in spectra] + [x * cs for x in spectra]
-                rows = jnp.concatenate([x.astype(jnp.bfloat16) for x in _pairs(rows)], 0)
-                sums[offset] += jnp.dot(
-                    rows, now.astype(jnp.bfloat16), preferred_element_type=jnp.float32
-                )
-                before, now = now, twice * now - before
+                at = pl.multiple_of((owner * SPIN_DEV + offset) * (2 * beams), 2 * beams)
+                values = spec[tile, pl.ds(at, 2 * beams)]
+                for half, wave in enumerate((cc, cs)):
+                    for pair in range(beams):
+                        rows = [
+                            jnp.broadcast_to(values[row : row + 1], (8, 128)) * wave
+                            for row in (2 * pair, 2 * pair + 1)
+                        ]
+                        place = (half * beams + pair) * 16
+                        left[offset, place : place + 16, lanes] = jnp.concatenate(rows, 0).astype(
+                            jnp.bfloat16
+                        )
                 cc, cs = cc * turn_c - cs * turn_s, cs * turn_c + cc * turn_s
-            fine[0, lanes], fine[1, lanes] = before, now
             coarse[0, :, lanes], coarse[1, :, lanes] = cc, cs
-        return sums
+            for piece in range(start, start + 128, 64):
+                rows = slice(piece, piece + 64)
+                before, now, twice = fine[0, rows], fine[1, rows], fine[2, rows]
+                for offset in range(SPIN_DEV):
+                    right[offset, rows] = now.astype(jnp.bfloat16)
+                    before, now = now, twice * now - before
+                fine[0, rows], fine[1, rows] = before, now
+
+    def multiply(left, right):
+        return [
+            jnp.dot(left[offset], right[offset], preferred_element_type=jnp.float32)
+            for offset in range(SPIN_DEV)
+        ]
 
     @pl.when(step == steps - 1)
     def _():
@@ -132,19 +148,22 @@
         mask = jnp.where(coarse_hit, scale, 0.0)
         signed = jnp.where(coarse_hit, scale * coarse_sign, 0.0)
 
-        def pick_bin(sums):
+        def pick_owner(left, right):
+            sums = jnp.concatenate(multiply(left, right), 0)
             high = sums.astype(jnp.bfloat16)
             low = (sums - high.astype(jnp.float32)).astype(jnp.bfloat16)
             picked = jnp.dot(
                 jnp.concatenate([high, low], 1), pick, preferred_element_type=jnp.float32
             )
-            parts = picked.reshape(2, 2, beams, COARSE, 2 * count)
-            cc, cs = parts[0, ..., :count], parts[0, ..., count:]
-            sc, ss = parts[1, ..., :count], parts[1, ..., count:]
-            real = (cc[0] - cs[1]) * mask - (ss[0] + sc[1]) * signed
-            imag = (cs[0] + cc[1]) * mask + (sc[0] - ss[1]) * signed
-            real, imag = jnp.sum(real, axis=1), jnp.sum(imag, axis=1)
-            return jnp.concatenate([real, imag], 0)
+            parts = picked.reshape(SPIN_DEV, 2, 2, beams, COARSE, 2 * count)
+            out = []
+            for offset in range(SPIN_DEV):
+                cc, cs = parts[offset, 0, ..., :count], parts[offset, 0, ..., count:]
+                sc, ss = parts[offset, 1, ..., :count], parts[offset, 1, ..., count:]
+                real = (cc[0] - cs[1]) * mask - (ss[0] + sc[1]) * signed
+                imag = (cs[0] + cc[1]) * mask + (sc[0] - ss[1]) * signed
+                out.append(jnp.concatenate([jnp.sum(real, axis=1), jnp.sum(imag, axis=1)], 0))
+            return out
 
         pairs = n // 2
         side = lax.rem(me, 2)
@@ -198,8 +217,10 @@
                 to_owner(pair, my_pair).start()
 
         def one_pair(pair, carry):
-            even = [pick_bin(sums) for sums in owner_sums(2 * pair)]
-            odd = [pick_bin(sums) for sums in owner_sums(2 * pair + 1)]
+            build(2 * pair + 1, left_b, right_b)
+            even = pick_owner(left_a, right_a)
+            build(lax.rem(2 * pair + 2, n), left_a, right_a)
+            odd = pick_owner(left_b, right_b)
             for offset in range(SPIN_DEV):
                 give[pair, offset] = jnp.where(side == 0, odd[offset], even[offset])
                 mine[pair, offset] = jnp.where(side == 0, even[offset], odd[offset])
@@ -211,6 +232,7 @@
 
             return carry
 
+        build(0, left_a, right_a)
         lax.fori_loop(0, pairs, one_pair, 0)
         pass_on(pairs - 1)
 
@@ -263,10 +285,6 @@
     for index in range(128 // lanes):
         total = jnp.where(place == index, power[:, index * lanes : (index + 1) * lanes], total)
     own_ref[...] = total
-
-
-def _pairs(rows):
-    return [jnp.concatenate(rows[i : i + 2], 0) for i in range(0, len(rows), 2)]
 
 
 def per_device(voltages, delay_step, trials):
@@ -299,9 +317,13 @@
             pl.BlockSpec((beams, 128), lambda i: (0, 0)),
         ),
         scratch_shapes=[
-            vmem((rows, bins, local_chan), jnp.float32),
+            vmem((local_chan // 128, bins * rows, 128), jnp.float32),
             vmem((3, local_chan, 2 * FINE), jnp.float32),
             vmem((4, COARSE, local_chan), jnp.float32),
+            vmem((SPIN_DEV, 2 * rows * COARSE, local_chan), jnp.bfloat16),
+            vmem((SPIN_DEV, local_chan, 2 * FINE), jnp.bfloat16),
+            vmem((SPIN_DEV, 2 * rows * COARSE, local_chan), jnp.bfloat16),
+            vmem((SPIN_DEV, local_chan, 2 * FINE), jnp.bfloat16),
             vmem((n // 2, SPIN_DEV, rows, count), jnp.float32),
             vmem((n // 2, SPIN_DEV, rows, count), jnp.float32),
             vmem((n // 2, SPIN_DEV, rows, count), jnp.float32),

time: 34.1 us -> 36.9 us (1.082)
  Pallas kernels: 33.3 us -> 36.1 us
    pallas_call x1, Pallas kernels: 31.4 us -> 34.2 us  [per_device(): pl.pallas_call(functools.partial(kernel, n, bins, chan_total), out_shape=...]
where the time goes in v3:
time: 36.9 us; the launch traced here: 36.7 us
  Pallas kernels  36.1 us (98%)
  between operations  0.64 us (2%)
    pallas_call x1, Pallas kernels, per_device(): pl.pallas_call(functools.partial(kernel, n, bins, chan_total), out_shape=...  34.2 us
    pallas_call x1, Pallas kernels, per_device(): pl.pallas_call(functools.partial(finish_kernel, n), out_shape=(jax.ShapeD...  1.87 us

profile of v3, /device:TPU:0, one launch (start us, length us, event | category | flops | bytes accessed | tf_op | source)
XLA Modules:
  0.0 36.7 jit_solution(4482172072084775338)
XLA Ops:
  0.6 34.2 %shard_map.59 = (f32[3,8,256]{2,1,0:T(8,128)}, f32[4,128]{1,0:T(4,128)}) custom-call(bf16[4,1024,2048]{2,1,0:T(8,128)(2,1)} %v_ref.1, bf16[2048,128]{1,0:T(8,128)(2,1)} %constant.2.clone.table_ref, s32[1,16384]{1,0:T(1,128)} %bitcast.2, s32[1,256]{1,0:T(1,128)} %bitcast.3), custom_call_target="tpu_custom_call" | custom-call | tf_op jit(solution)/shard_map/pallas_call | solution.py:302
  34.9 1.9 %shard_map.60 = (f32[3,2,4,256]{3,2,1,0:T(4,128)}, f32[4,16]{1,0:T(4,128)}) custom-call(f32[3,8,256]{2,1,0:T(8,128)} %get-tuple-element.4.spectra_ref, f32[4,128]{1,0:T(4,128)} %get-tuple-element.5.power_ref), custom_call_target="tpu_custom_call" | custom-call | tf_op jit(solution)/shard_map/pallas_call | solution.py:348

commit v4 on v2

--- a/solution.py
+++ b/solution.py
@@ -72,8 +72,11 @@
         rows = jnp.dot(v_ref[beam], table_ref[...], preferred_element_type=jnp.float32)
         rows = (rows.T * (1.0 / math.sqrt(samples))).astype(jnp.bfloat16).astype(jnp.float32)
         real, imag = rows[:bins], rows[bins : 2 * bins]
-        spec[beam, :, here] = real * mid_cos - imag * mid_sin
-        spec[beams + beam, :, here] = real * mid_sin + imag * mid_cos
+        turned = real * mid_cos - imag * mid_sin, real * mid_sin + imag * mid_cos
+        for kind, values in enumerate(turned):
+            place = pl.ds(kind * beams + beam, bins, stride=2 * beams)
+            for tile in range(chunk // 128):
+                spec[step * (chunk // 128) + tile, place, :] = values[:, tile * 128 : tile * 128 + 128]
 
     column = jnp.broadcast_to(delay_ref[...].astype(jnp.float32), (2 * FINE, chunk)).T
     lane = lax.broadcasted_iota(jnp.int32, (chunk, 2 * FINE), 1)
@@ -91,15 +94,17 @@
 
     def owner_sums(owner):
         sums = [0.0] * SPIN_DEV
-        for block in range(spec.shape[2] // chunk):
+        for block in range(spec.shape[0] * 128 // chunk):
             lanes = slice(block * chunk, (block + 1) * chunk)
             before, now, twice = fine[0, lanes], fine[1, lanes], fine[2, lanes]
             cc, cs, turn_c, turn_s = (coarse[index, :, lanes] for index in range(4))
             for offset in range(SPIN_DEV):
                 spin_bin = owner * SPIN_DEV + offset
+                at = pl.multiple_of(spin_bin * (2 * beams), 2 * beams)
+                tiles = range(block * chunk // 128, (block + 1) * chunk // 128)
+                values = jnp.concatenate([spec[tile, pl.ds(at, 2 * beams)] for tile in tiles], 1)
                 spectra = [
-                    jnp.broadcast_to(spec[row, pl.ds(spin_bin, 1), lanes], (8, chunk))
-                    for row in range(2 * beams)
+                    jnp.broadcast_to(values[row : row + 1], (8, chunk)) for row in range(2 * beams)
                 ]
                 rows = [x * cc for x in spectra] + [x * cs for x in spectra]
                 rows = jnp.concatenate([x.astype(jnp.bfloat16) for x in _pairs(rows)], 0)
@@ -299,7 +304,7 @@
             pl.BlockSpec((beams, 128), lambda i: (0, 0)),
         ),
         scratch_shapes=[
-            vmem((rows, bins, local_chan), jnp.float32),
+            vmem((local_chan // 128, bins * rows, 128), jnp.float32),
             vmem((3, local_chan, 2 * FINE), jnp.float32),
             vmem((4, COARSE, local_chan), jnp.float32),
             vmem((n // 2, SPIN_DEV, rows, count), jnp.float32),

time: 34.1 us -> 34.2 us (level)
  no operation moved by 1% of the time
where the time goes in v4:
time: 34.2 us; the launch traced here: 34 us
  Pallas kernels  33.4 us (98%)
  between operations  0.64 us (2%)
    pallas_call x1, Pallas kernels, per_device(): pl.pallas_call(functools.partial(kernel, n, bins, chan_total), out_shape=...  31.5 us
    pallas_call x1, Pallas kernels, per_device(): pl.pallas_call(functools.partial(finish_kernel, n), out_shape=(jax.ShapeD...  1.87 us

profile of v4, /device:TPU:0, one launch (start us, length us, event | category | flops | bytes accessed | tf_op | source)
XLA Modules:
  0.0 34.0 jit_solution(16580031374254965018)
XLA Ops:
  0.6 31.5 %shard_map.59 = (f32[3,8,256]{2,1,0:T(8,128)}, f32[4,128]{1,0:T(4,128)}) custom-call(bf16[4,1024,2048]{2,1,0:T(8,128)(2,1)} %v_ref.1, bf16[2048,128]{1,0:T(8,128)(2,1)} %constant.2.clone.table_ref, s32[1,16384]{1,0:T(1,128)} %bitcast.2, s32[1,256]{1,0:T(1,128)} %bitcast.3), custom_call_target="tpu_custom_call" | custom-call | tf_op jit(solution)/shard_map/pallas_call | solution.py:289
  32.1 1.9 %shard_map.60 = (f32[3,2,4,256]{3,2,1,0:T(4,128)}, f32[4,16]{1,0:T(4,128)}) custom-call(f32[3,8,256]{2,1,0:T(8,128)} %get-tuple-element.4.spectra_ref, f32[4,128]{1,0:T(4,128)} %get-tuple-element.5.power_ref), custom_call_target="tpu_custom_call" | custom-call | tf_op jit(solution)/shard_map/pallas_call | solution.py:331

commit v5 on v2

--- a/solution.py
+++ b/solution.py
@@ -132,19 +132,22 @@
         mask = jnp.where(coarse_hit, scale, 0.0)
         signed = jnp.where(coarse_hit, scale * coarse_sign, 0.0)
 
-        def pick_bin(sums):
+        def pick_owner(owner):
+            sums = jnp.concatenate(owner_sums(owner), 0)
             high = sums.astype(jnp.bfloat16)
             low = (sums - high.astype(jnp.float32)).astype(jnp.bfloat16)
             picked = jnp.dot(
                 jnp.concatenate([high, low], 1), pick, preferred_element_type=jnp.float32
             )
-            parts = picked.reshape(2, 2, beams, COARSE, 2 * count)
-            cc, cs = parts[0, ..., :count], parts[0, ..., count:]
-            sc, ss = parts[1, ..., :count], parts[1, ..., count:]
-            real = (cc[0] - cs[1]) * mask - (ss[0] + sc[1]) * signed
-            imag = (cs[0] + cc[1]) * mask + (sc[0] - ss[1]) * signed
-            real, imag = jnp.sum(real, axis=1), jnp.sum(imag, axis=1)
-            return jnp.concatenate([real, imag], 0)
+            parts = picked.reshape(SPIN_DEV, 2, 2, beams, COARSE, 2 * count)
+            out = []
+            for offset in range(SPIN_DEV):
+                cc, cs = parts[offset, 0, ..., :count], parts[offset, 0, ..., count:]
+                sc, ss = parts[offset, 1, ..., :count], parts[offset, 1, ..., count:]
+                real = (cc[0] - cs[1]) * mask - (ss[0] + sc[1]) * signed
+                imag = (cs[0] + cc[1]) * mask + (sc[0] - ss[1]) * signed
+                out.append(jnp.concatenate([jnp.sum(real, axis=1), jnp.sum(imag, axis=1)], 0))
+            return out
 
         pairs = n // 2
         side = lax.rem(me, 2)
@@ -198,8 +201,8 @@
                 to_owner(pair, my_pair).start()
 
         def one_pair(pair, carry):
-            even = [pick_bin(sums) for sums in owner_sums(2 * pair)]
-            odd = [pick_bin(sums) for sums in owner_sums(2 * pair + 1)]
+            even = pick_owner(2 * pair)
+            odd = pick_owner(2 * pair + 1)
             for offset in range(SPIN_DEV):
                 give[pair, offset] = jnp.where(side == 0, odd[offset], even[offset])
                 mine[pair, offset] = jnp.where(side == 0, even[offset], odd[offset])

time: 34.1 us -> 35 us (1.026)
  Pallas kernels: 33.3 us -> 34.2 us
    pallas_call x1, Pallas kernels: 31.4 us -> 32.4 us  [per_device(): pl.pallas_call(functools.partial(kernel, n, bins, chan_total), out_shape=...]
where the time goes in v5:
time: 35 us; the launch traced here: 34.9 us
  Pallas kernels  34.2 us (98%)
  between operations  0.64 us (2%)
    pallas_call x1, Pallas kernels, per_device(): pl.pallas_call(functools.partial(kernel, n, bins, chan_total), out_shape=...  32.4 us
    pallas_call x1, Pallas kernels, per_device(): pl.pallas_call(functools.partial(finish_kernel, n), out_shape=(jax.ShapeD...  1.87 us

profile of v5, /device:TPU:0, one launch (start us, length us, event | category | flops | bytes accessed | tf_op | source)
XLA Modules:
  0.0 34.9 jit_solution(7097191427111501652)
XLA Ops:
  0.6 32.4 %shard_map.59 = (f32[3,8,256]{2,1,0:T(8,128)}, f32[4,128]{1,0:T(4,128)}) custom-call(bf16[4,1024,2048]{2,1,0:T(8,128)(2,1)} %v_ref.1, bf16[2048,128]{1,0:T(8,128)(2,1)} %constant.2.clone.table_ref, s32[1,16384]{1,0:T(1,128)} %bitcast.2, s32[1,256]{1,0:T(1,128)} %bitcast.3), custom_call_target="tpu_custom_call" | custom-call | tf_op jit(solution)/shard_map/pallas_call | solution.py:287
  33.0 1.9 %shard_map.60 = (f32[3,2,4,256]{3,2,1,0:T(4,128)}, f32[4,16]{1,0:T(4,128)}) custom-call(f32[3,8,256]{2,1,0:T(8,128)} %get-tuple-element.4.spectra_ref, f32[4,128]{1,0:T(4,128)} %get-tuple-element.5.power_ref), custom_call_target="tpu_custom_call" | custom-call | tf_op jit(solution)/shard_map/pallas_call | solution.py:329
